TPU v7x, 512 devices: a whole 4x4x16 slice. The times are simulated.
512 devices in a mesh: fsdp: 32 (over x_lo, z), side: 16 (over y, x_hi, core).
Axes of the slice: x: 4 (x_hi: 2, x_lo: 2; x = x_hi * 2 + x_lo), y: 4, z: 16, core: 2. Of those that a mesh axis runs over, the one named last changes fastest.
Arguments:
- attn_inputs: bfloat16 [65536, 5120], P(('side', 'fsdp')), may hold values from -24 to 24
- queries: bfloat16 [65536, 2560], P(('side', 'fsdp')), may hold values from -310 to 310
- key_vectors: bfloat16 [65536, 512], P(('side', 'fsdp')), may hold values from -12 to 12
- logp_grad: bfloat16 [65536, 2560], P(('side', 'fsdp')), may hold values from -24 to 24
- new_logp: float32 [65536], P(('side', 'fsdp')), may hold values from -6.5 to -0.01
- old_logp: float32 [65536], P(('side', 'fsdp')), may hold values from -4 to -0.05
- rewards: float32 [32], replicated, may hold values from -8 to 8
- group_ids: int32 [32], replicated, may hold values from 0 to 7
- lengths: int32 [32], replicated, may hold values from 1024 to 2048
- value_proj: bfloat16 [5120, 512], P('fsdp'), may hold values from -0.078125 to 0.078125
- first_moment: bfloat16 [5120, 512], P(('fsdp', 'side')), may hold values from -120 to 120
- second_moment: bfloat16 [5120, 512], P(('fsdp', 'side')), may hold values from 100 to 9984
Outputs:
- input_grad: bfloat16 [65536, 5120], P(('side', 'fsdp'))
- new_proj: bfloat16 [5120, 512], P('fsdp')
- new_first: bfloat16 [5120, 512], P(('fsdp', 'side'))
- new_second: bfloat16 [5120, 512], P(('fsdp', 'side'))
All inputs are finite; a program needn't handle non-finite values.
Results may differ from a plain program's by a relative error of at most 0.03.
Values may be sent and summed in bfloat16 or wider, within the bound.
A program may use at most 64 MiB of HBM per device.

v0:
```python
import math
import jax
import jax.numpy as jnp
from jax import lax
from jax.sharding import Mesh
from jax.sharding import PartitionSpec as P

QH = 20
KVH = 4
HEAD = 128
ROLLS = 2
FSDP = ("fsdp_0", "fsdp_1")
SIDE_FSDP = ("side", "fsdp_0", "fsdp_1")
FSDP_SIDE = ("fsdp_0", "fsdp_1", "side")
clip_low = 0.8
clip_high = 1.2
decay_first = 0.9
decay_second = 0.95
step_rate = 0.001
weight_decay = 0.1
adam_eps = 1e-08
bias_first = 1.0 - 0.9**10
bias_second = 1.0 - 0.95**10


def laid_out(pieces, dim):
    pieces = jnp.moveaxis(pieces, 0, dim)
    dims = pieces.shape
    return pieces.reshape(*dims[:dim], dims[dim] * dims[dim + 1], *dims[dim + 2 :])


def all_blocks(value, axes, sequence):
    pieces = value
    for k in sequence:
        pieces = lax.all_gather(pieces, axes[k])
    done = sequence[::-1]
    back = [done.index(k) for k in range(len(axes))]
    pieces = pieces.transpose(*back, *range(len(axes), pieces.ndim))
    return pieces.reshape(-1, *value.shape)


def whole_of(value, axes, sequence, dim):
    return laid_out(all_blocks(value, axes, sequence), dim)


def reduced_to_own(pieces, axes, sequence):
    dims = [lax.axis_size(a) for a in axes]
    pieces = pieces.reshape(*dims, *pieces.shape[1:])
    pieces = pieces.transpose(*sequence, *range(len(axes), pieces.ndim))
    pieces = pieces.reshape(-1, *pieces.shape[len(axes) :])
    for k in sequence:
        pieces = lax.psum_scatter(pieces, axes[k], scatter_dimension=0, tiled=True)
    return pieces[0]


def split_up(value, dim, peers):
    before, after = (value.shape[:dim], value.shape[dim + 1 :])
    return jnp.moveaxis(value.reshape(*before, peers, -1, *after), dim, 0)


def summed_rows(value, axes, sequence, dim):
    peers = lax.axis_size(axes)
    return reduced_to_own(split_up(value, dim, peers), axes, sequence)


def sum_at_owner(value, axis, dim):
    pieces = split_up(value, dim, lax.axis_size(axis))
    arrived = lax.all_to_all(pieces, axis, split_axis=0, concat_axis=0, tiled=True)
    return arrived.astype(jnp.float32).sum(axis=0)


def from_everyone(value, axis):
    peers = lax.axis_size(axis)
    return lax.all_to_all(
        jnp.broadcast_to(value[None], (peers, *value.shape)), axis, 0, 0, tiled=True
    )


def collect(value, axis, dim):
    pieces = from_everyone(value, axis)
    return laid_out(pieces, dim)


def advantages(rewards, group_ids):
    group_count = rewards.shape[0] // 4
    member = (group_ids[:, None] == jnp.arange(group_count, dtype=jnp.int32)[None, :]).astype(
        jnp.float32
    )
    counts = jnp.maximum(jnp.sum(member, axis=0), 1.0)
    group_mean = jnp.sum(member * rewards[:, None], axis=0) / counts
    own_mean = jnp.sum(member * group_mean[None, :], axis=1)
    spread = rewards - own_mean
    variance = jnp.sum(member * (spread * spread)[:, None], axis=0) / counts
    own_std = jnp.sqrt(jnp.sum(member * variance[None, :], axis=1))
    return spread / jnp.maximum(own_std, 1.0)


def coefficient(new_lp, old_lp, adv_tok, len_tok, pos_tok, full_len):
    ratio_now = jnp.exp(new_lp - old_lp)
    clipped = jnp.clip(ratio_now, clip_low, clip_high)
    active = (ratio_now * adv_tok <= clipped * adv_tok) & (pos_tok < len_tok)
    len_weight = full_len / len_tok.astype(jnp.float32)
    return jnp.where(active, -adv_tok * ratio_now * len_weight, 0.0)


def block_values(query_blk, grad_blk, roll_keys, first_pos):
    tok_rows = query_blk.shape[0]
    key_count = roll_keys.shape[0]
    per_group = QH // KVH
    score_scale = 1.0 / math.sqrt(HEAD)
    query_pos = first_pos + jnp.arange(tok_rows, dtype=jnp.int32)
    key_pos = jnp.arange(key_count, dtype=jnp.int32)
    allowed = jnp.tile(key_pos[None, :] <= query_pos[:, None], (per_group, 1))
    pieces = []
    for kv_head in range(KVH):
        col_low = kv_head * per_group * HEAD
        col_high = col_low + per_group * HEAD
        q_part = (
            query_blk[:, col_low:col_high]
            .reshape(tok_rows, per_group, HEAD)
            .transpose(1, 0, 2)
            .reshape(per_group * tok_rows, HEAD)
        )
        g_part = (
            grad_blk[:, col_low:col_high]
            .reshape(tok_rows, per_group, HEAD)
            .transpose(1, 0, 2)
            .reshape(per_group * tok_rows, HEAD)
        )
        k_part = roll_keys[:, kv_head * HEAD : (kv_head + 1) * HEAD]
        scores = jnp.dot(q_part, k_part.T, preferred_element_type=jnp.float32) * score_scale
        scores = jnp.where(allowed, scores, -1e30)
        top_val = jnp.max(scores, axis=1, keepdims=True)
        expo = jnp.exp(scores - top_val)
        attention = (expo / jnp.sum(expo, axis=1, keepdims=True)).astype(jnp.bfloat16)
        pieces.append(jnp.dot(attention.T, g_part, preferred_element_type=jnp.float32))
    return jnp.concatenate(pieces, axis=1)


def adam_rows(old_rows, grad_rows, first_moment, second_moment):
    first = decay_first * first_moment.astype(jnp.float32) + (1.0 - decay_first) * grad_rows
    second = (
        decay_second * second_moment.astype(jnp.float32)
        + (1.0 - decay_second) * grad_rows * grad_rows
    )
    weight_now = old_rows.astype(jnp.float32)
    update = (
        first / bias_first / (jnp.sqrt(second / bias_second) + adam_eps) + weight_decay * weight_now
    )
    return (
        (weight_now - step_rate * update).astype(jnp.bfloat16),
        first.astype(jnp.bfloat16),
        second.astype(jnp.bfloat16),
    )


def shards(
    attn_inputs,
    queries,
    key_vectors,
    logp_grad,
    new_logp,
    old_logp,
    rewards,
    group_ids,
    lengths,
    value_proj,
    first_moment,
    second_moment,
):
    fsdp_size = lax.axis_size(FSDP)
    fsdp_index = lax.axis_index(FSDP)
    side_index = lax.axis_index("side")
    tok_rows = attn_inputs.shape[0]
    half = tok_rows // ROLLS
    full_len = half * fsdp_size
    width = key_vectors.shape[1]
    first_pos = fsdp_index * half
    advantage = advantages(rewards, group_ids)
    slot = jnp.arange(tok_rows, dtype=jnp.int32)
    global_roll = side_index * ROLLS + slot // half
    position = first_pos + slot % half
    coeff = coefficient(
        new_logp, old_logp, advantage[global_roll], lengths[global_roll], position, full_len
    )
    out_grad = (coeff[:, None] * logp_grad.astype(jnp.float32)).astype(jnp.bfloat16)
    in_columns = lax.all_to_all(attn_inputs, FSDP, split_axis=1, concat_axis=0, tiled=True)
    all_keys = whole_of(key_vectors, FSDP, (0, 1), 0)
    keys_split = all_keys.reshape(fsdp_size, ROLLS, half, width)
    partials = []
    for roll in range(ROLLS):
        roll_keys = keys_split[:, roll].reshape(full_len, width)
        partials.append(
            block_values(
                queries[roll * half : (roll + 1) * half],
                out_grad[roll * half : (roll + 1) * half],
                roll_keys,
                first_pos,
            )
        )
    stacked = jnp.stack(partials, axis=0)
    placed = (
        stacked.reshape(ROLLS, fsdp_size, half, width)
        .transpose(1, 0, 2, 3)
        .reshape(fsdp_size * tok_rows, width)
    )
    own_grad = (
        summed_rows(placed.astype(jnp.bfloat16), FSDP, (1, 0), 0)
        .astype(jnp.float32)
        .astype(jnp.bfloat16)
    )
    values_grad = lax.all_gather(own_grad, FSDP, axis=0, tiled=True)
    grad_cols = jnp.dot(values_grad, value_proj.T, preferred_element_type=jnp.float32).astype(
        jnp.bfloat16
    )
    input_grad = lax.all_to_all(grad_cols, FSDP, split_axis=0, concat_axis=1, tiled=True)
    weight_grad = lax.dot_general(
        in_columns, values_grad, (((0,), (0,)), ((), ())), preferred_element_type=jnp.float32
    )
    shard_grad = sum_at_owner(weight_grad.astype(jnp.bfloat16), "side", 0)
    shard_rows = shard_grad.shape[0]
    old_rows = lax.dynamic_slice_in_dim(value_proj, side_index * shard_rows, shard_rows, 0)
    new_rows, new_first, new_second = adam_rows(old_rows, shard_grad, first_moment, second_moment)
    new_proj = collect(new_rows, "side", 0)
    return (input_grad, new_proj, new_first, new_second)


def solution(mesh):
    torus = Mesh(mesh.devices.reshape(2, 16, mesh.shape["side"]), ("fsdp_0", "fsdp_1", "side"))
    placed = (
        P(SIDE_FSDP, None),
        P(SIDE_FSDP, None),
        P(SIDE_FSDP, None),
        P(SIDE_FSDP, None),
        P(SIDE_FSDP),
        P(SIDE_FSDP),
        P(),
        P(),
        P(),
        P(FSDP, None),
        P(FSDP_SIDE, None),
        P(FSDP_SIDE, None),
    )
    return jax.shard_map(
        shards,
        mesh=torus,
        in_specs=placed,
        out_specs=(P(SIDE_FSDP, None), P(FSDP, None), P(FSDP_SIDE, None), P(FSDP_SIDE, None)),
        check_vma=False,
    )
```

profile of v0, /device:TPU:32, one launch (start us, length us, event | category | flops | bytes accessed | tf_op | source)
XLA Modules:
  0.0 514.3 jit_solution(6397335464819392959)
XLA Ops:
  7.3 7.6 %all-gather = bf16[256,512]{1,0:T(8,128)(2,1)} all-gather(bf16[128,512]{1,0:T(8,128)(2,1)} %param.14), channel_id=2, replica_groups=mesh['fsdp_0'=2,'fsdp_1'=16,'side'=16] {'fsdp_0'}, dimensions={0}, use_global_device_ids=true | all-gather | bytes 393216 | tf_op jit(solution)/shard_map/all_gather | solution.py:35
  15.0 1.2 fusion.53
  20.2 1.2 gather_fusion
  30.1 67.4 %all-gather.6.cloned.1.call-done = bf16[32,128,512]{2,1,0:T(8,128)(2,1)} async-done(((bf16[2,128,512]{2,1,0:T(8,128)(2,1)}), bf16[32,128,512]{2,1,0:T(8,128)(2,1)}) %all-gather.6.cloned.1.call-update) | async-done | bytes 4194320 | tf_op jit(solution)/shard_map/all_gather | solution.py:35
  97.5 2.6 copy.92
  109.8 1.5 pad_maximum_fusion
  111.3 3.9 copy.100
  124.5 2.6 copy.109
  127.1 2.6 maximum_bitcast_fusion
  130.2 2.4 copy.111
  132.6 75.9 %reduce-scatter.3.cloned.1.call-done = bf16[2,128,512]{2,1,0:T(8,128)(2,1)} async-done(((bf16[32,128,512]{2,1,0:T(8,128)(2,1)}), bf16[2,128,512]{2,1,0:T(8,128)(2,1)}) %reduce-scatter.3.cloned.1.call-update) | async-done | bytes 262160 | tf_op jit(solution)/shard_map/reduce_scatter | solution.py:52
  208.6 23.0 %reduce-scatter.5.cloned.1.call-done = bf16[1,128,512]{2,1,0:T(8,128)(2,1)} async-done(((bf16[2,128,512]{2,1,0:T(8,128)(2,1)}), bf16[1,128,512]{2,1,0:T(8,128)(2,1)}) %reduce-scatter.5.cloned.1.call-update) | async-done | bytes 131088 | tf_op jit(solution)/shard_map/reduce_scatter | solution.py:52
  232.4 91.0 %all_to_all.48 = bf16[128,32,160]{0,2,1:T(8,128)(2,1)S(1)} all-to-all(bf16[128,32,160]{0,2,1:T(8,128)(2,1)S(1)} %bitcast.123), channel_id=1, replica_groups=mesh['fsdp_0'=2,'fsdp_1'=16,'side'=16] {'fsdp_0','fsdp_1'}, dimensions={1} | all-to-all | bytes 2621440 | tf_op jit(solution)/shard_map/all_to_all | solution.py:187
  323.4 77.8 %all-gather.8.cloned.1.call-done = bf16[1,4096,512]{2,1,0:T(8,128)(2,1)} async-done(((bf16[1,128,512]{2,1,0:T(8,128)(2,1)}), bf16[1,4096,512]{2,1,0:T(8,128)(2,1)}) %all-gather.8.cloned.1.call-update) | async-done | bytes 4194320 | tf_op jit(solution)/shard_map/all_gather | solution.py:212
  401.2 3.0 fusion.29
  405.0 6.4 %all-to-all-start.2 = ((bf16[16,10,512]{2,1,0:T(8,128)(2,1)}), bf16[16,10,512]{2,1,0:T(8,128)(2,1)S(1)}, u32[]{:S(2)}, u32[]{:S(2)}) async-start(bf16[16,10,512]{2,1,0:T(8,128)(2,1)} %reshape.265), calls=%async_computation.4 | async-start | bytes 524288 | tf_op jit(solution)/shard_map/all_to_all | solution.py:68
  411.4 9.6 %all-to-all-done.2 = bf16[16,10,512]{2,1,0:T(8,128)(2,1)S(1)} async-done(((bf16[16,10,512]{2,1,0:T(8,128)(2,1)}), bf16[16,10,512]{2,1,0:T(8,128)(2,1)S(1)}, u32[]{:S(2)}, u32[]{:S(2)}) %all-to-all-start.2) | async-done | bytes 163872 | tf_op jit(solution)/shard_map/all_to_all | solution.py:68
  422.4 3.5 all-to-all-start.3
  426.0 3.7 fusion.19
  429.7 1.3 copy.127
  430.9 4.5 all-to-all-done.3
  435.5 6.1 %all-to-all-start = ((bf16[32,128,160]{1,2,0:T(8,128)(2,1)}), bf16[32,128,160]{1,2,0:T(8,128)(2,1)S(1)}, u32[]{:S(2)}, u32[]{:S(2)}) async-start(bf16[32,128,160]{1,2,0:T(8,128)(2,1)} %bitcast.100), calls=%async_computation.2 | async-start | bytes 2621440 | tf_op jit(solution)/shard_map/all_to_all | solution.py:216
  442.3 64.1 %all-to-all-done = bf16[32,128,160]{1,2,0:T(8,128)(2,1)S(1)} async-done(((bf16[32,128,160]{1,2,0:T(8,128)(2,1)}), bf16[32,128,160]{1,2,0:T(8,128)(2,1)S(1)}, u32[]{:S(2)}, u32[]{:S(2)}) %all-to-all-start) | async-done | bytes 1310752 | tf_op jit(solution)/shard_map/all_to_all | solution.py:216
  506.3 1.4 copy.115
  (124 shorter events, 35.7 us)
Async XLA Ops:
  7.2 14.2 %copy-start = (s32[32]{0:T(128)S(1)}, s32[32]{0:T(128)}, u32[]{:S(2)}) copy-start(s32[32]{0:T(128)} %param.20) | copy-start | bytes 388
  7.2 15.5 %copy-start.15 = (f32[128]{0:T(128)S(1)}, f32[128]{0:T(128)}, u32[]{:S(2)}) copy-start(f32[128]{0:T(128)} %param.16) | copy-start | bytes 1540
  7.2 15.5 %copy-start.16 = (f32[128]{0:T(128)S(1)}, f32[128]{0:T(128)}, u32[]{:S(2)}) copy-start(f32[128]{0:T(128)} %param.17) | copy-start | bytes 1540
  7.2 15.5 %copy-start.3 = (bf16[128,2560]{1,0:T(8,128)(2,1)S(1)}, bf16[128,2560]{1,0:T(8,128)(2,1)}, u32[]{:S(2)}) copy-start(bf16[128,2560]{1,0:T(8,128)(2,1)} %param.15) | copy-start | bytes 1966084
  7.2 90.3 %all-gather.6.cloned.1.call-start = ((), (), s32[]{:S(2)}) async-start(), calls=%async_computation.8 | async-start | bytes 4456448 | tf_op jit(solution)/shard_map/all_gather | solution.py:35
  14.9 193.6 %reduce-scatter.3.cloned.1.call-start = ((), (), s32[]{:S(2)}) async-start(), calls=%async_computation.6 | async-start | bytes 4456448 | tf_op jit(solution)/shard_map/reduce_scatter | solution.py:52
  102.9 1.3 copy-start.9
  104.9 0.9 copy-start.10
  106.6 0.9 copy-start.11
  108.2 0.9 copy-start.12
  117.4 1.2 copy-start.5
  119.4 0.9 copy-start.6
  121.0 0.9 copy-start.7
  122.7 0.9 copy-start.8
  132.6 99.1 %copy-start.2 = (bf16[128,5120]{1,0:T(8,128)(2,1)S(1)}, bf16[128,5120]{1,0:T(8,128)(2,1)}, u32[]{:S(2)}) copy-start(bf16[128,5120]{1,0:T(8,128)(2,1)} %param.12) | copy-start | bytes 3932164
  132.6 99.0 %reduce-scatter.5.cloned.1.call-start = ((), (), s32[]{:S(2)}) async-start(), calls=%async_computation.7 | async-start | bytes 393216 | tf_op jit(solution)/shard_map/reduce_scatter | solution.py:52
  208.5 192.7 %all-gather.8.cloned.1.call-start = ((), (), s32[]{:S(2)}) async-start(), calls=%async_computation.9 | async-start | bytes 4325376 | tf_op jit(solution)/shard_map/all_gather | solution.py:212
  323.4 97.6 %copy-start.4 = (bf16[160,512]{1,0:T(8,128)(2,1)S(1)}, bf16[160,512]{1,0:T(8,128)(2,1)}, u32[]{:S(2)}) copy-start(bf16[160,512]{1,0:T(8,128)(2,1)} %param.21) | copy-start | bytes 491524
  323.4 97.6 %copy-start.13 = (bf16[10,512]{1,0:T(8,128)(2,1)S(1)}, bf16[10,512]{1,0:T(8,128)(2,1)}, u32[]{:S(2)}) copy-start(bf16[10,512]{1,0:T(8,128)(2,1)} %param.23) | copy-start | bytes 30724
  323.4 97.6 %copy-start.14 = (bf16[10,512]{1,0:T(8,128)(2,1)S(1)}, bf16[10,512]{1,0:T(8,128)(2,1)}, u32[]{:S(2)}) copy-start(bf16[10,512]{1,0:T(8,128)(2,1)} %param.22) | copy-start | bytes 30724
  405.0 16.0 %all-to-all-start.2 = ((bf16[16,10,512]{2,1,0:T(8,128)(2,1)}), bf16[16,10,512]{2,1,0:T(8,128)(2,1)S(1)}, u32[]{:S(2)}, u32[]{:S(2)}) async-start(bf16[16,10,512]{2,1,0:T(8,128)(2,1)} %reshape.265), calls=%async_computation.4 | async-start | bytes 524288 | tf_op jit(solution)/shard_map/all_to_all | solution.py:68
  422.4 13.1 %all-to-all-start.3 = ((bf16[16,10,512]{2,1,0:T(8,128)(2,1)}), bf16[16,10,512]{2,1,0:T(8,128)(2,1)S(1)}, u32[]{:S(2)}, u32[]{:S(2)}) async-start(bf16[16,10,512]{2,1,0:T(8,128)(2,1)} %broadcast_in_dim.19), calls=%async_computation.5 | async-start | bytes 524288 | tf_op jit(solution)/shard_map/all_to_all | solution.py:74
  435.5 72.3 %copy-start.1 = (s32[32]{0:T(128)S(1)}, s32[32]{0:T(128)}, u32[]{:S(2)}) copy-start(s32[32]{0:T(128)} %param.20) | copy-start | bytes 388
  435.5 70.9 %all-to-all-start = ((bf16[32,128,160]{1,2,0:T(8,128)(2,1)}), bf16[32,128,160]{1,2,0:T(8,128)(2,1)S(1)}, u32[]{:S(2)}, u32[]{:S(2)}) async-start(bf16[32,128,160]{1,2,0:T(8,128)(2,1)} %bitcast.100), calls=%async_computation.2 | async-start | bytes 2621440 | tf_op jit(solution)/shard_map/all_to_all | solution.py:216
Sparse Core Ops, SparseCore 0:
  15.0 82.4 all-gather.5
  132.7 75.7 reduce-scatter.2
  211.3 20.2 reduce-scatter.4
  233.7 167.3 all-gather.7
where the time goes:
time: 515 us; the launch traced here: 514 us
  waiting for transfers between devices  322 us (63%)
  blocking collectives  98.6 us (19%)
  local copies, waits for them, and re-layouts  31.3 us (6%)
  matrix products  18.5 us (4%)
  starting transfers between devices  16.2 us (3%)
  between operations  14.3 us (3%)
  other arithmetic  13.2 us (3%)
    reduce_scatter x2, waiting for transfers between devices, reduced_to_own(): pieces = lax.psum_scatter(pieces, axes[k], scatter_dimension=0, tiled=True)  98.9 us
    all_to_all x1, blocking collectives, shards(): lax.all_to_all(attn_inputs, FSDP, split_axis=1, concat_axis=0, tiled=True)  91 us
    all_gather x1, waiting for transfers between devices, shards(): values_grad = lax.all_gather(own_grad, FSDP, axis=0, tiled=True)  77.8 us
    all_gather x1, waiting for transfers between devices, all_blocks(): pieces = lax.all_gather(pieces, axes[k])  67.4 us
    all_to_all x1, waiting for transfers between devices, shards(): lax.all_to_all(grad_cols, FSDP, split_axis=0, concat_axis=1, tiled=True)  64.1 us
  transfers between devices with their start and end apart: 7, of which 7 were waited for; matrix products, arithmetic and copies ran while one was open for 4% of the time, Pallas kernels for 0%

commit v1 on v0

--- a/solution.py
+++ b/solution.py
@@ -21,6 +21,11 @@
 adam_eps = 1e-08
 bias_first = 1.0 - 0.9**10
 bias_second = 1.0 - 0.95**10
+
+
+def all_by_exchange(x, name, dim):
+    sent = jnp.stack([x] * lax.axis_size(name))
+    return jnp.concatenate(lax.all_to_all(sent, name, 0, 0), axis=dim)
 
 
 def laid_out(pieces, dim):
@@ -209,7 +214,7 @@
         .astype(jnp.float32)
         .astype(jnp.bfloat16)
     )
-    values_grad = lax.all_gather(own_grad, FSDP, axis=0, tiled=True)
+    values_grad = all_by_exchange(own_grad, FSDP, 0)
     grad_cols = jnp.dot(values_grad, value_proj.T, preferred_element_type=jnp.float32).astype(
         jnp.bfloat16
     )

time: 515 us -> 587 us (1.14)
  blocking collectives: 98.6 us -> 210 us
  waiting for transfers between devices: 322 us -> 272 us
  starting transfers between devices: 16.2 us -> 24 us
    all_to_all x1, blocking collectives: 91 us -> 202 us  [all_by_exchange(): return jnp.concatenate(lax.all_to_all(sent, name, 0, 0), axis=dim)]
    all_gather x1 -> x0, waiting for transfers between devices: 77.8 us -> none  [shards(): values_grad = lax.all_gather(own_grad, FSDP, axis=0, tiled=True)]
    reduce_scatter x2, waiting for transfers between devices: 98.9 us -> 127 us  [reduced_to_own(): pieces = lax.psum_scatter(pieces, axes[k], scatter_dimension=0, tiled=True)]
    all_to_all x0 -> x1, starting transfers between devices: none -> 9.01 us  [shards(): lax.all_to_all(attn_inputs, FSDP, split_axis=1, concat_axis=0, tiled=True)]
  transfers between devices with their start and end apart: 7 -> 7, of which waited for: 7 -> 6; matrix products, arithmetic and copies ran while one was open for 4% -> 4% of each run, Pallas kernels for 0% -> 0%
where the time goes in v1:
time: 587 us; the launch traced here: 586 us
  waiting for transfers between devices  272 us (46%)
  blocking collectives  210 us (36%)
  local copies, waits for them, and re-layouts  36.5 us (6%)
  starting transfers between devices  24 us (4%)
  matrix products  16.3 us (3%)
  between operations  14.3 us (2%)
  other arithmetic  13.2 us (2%)
    all_to_all x1, blocking collectives, all_by_exchange(): return jnp.concatenate(lax.all_to_all(sent, name, 0, 0), axis=dim)  202 us
    reduce_scatter x2, waiting for transfers between devices, reduced_to_own(): pieces = lax.psum_scatter(pieces, axes[k], scatter_dimension=0, tiled=True)  127 us
    all_gather x1, waiting for transfers between devices, all_blocks(): pieces = lax.all_gather(pieces, axes[k])  67.4 us
    all_to_all x1, waiting for transfers between devices, shards(): lax.all_to_all(grad_cols, FSDP, split_axis=0, concat_axis=1, tiled=True)  64.1 us
  transfers between devices with their start and end apart: 7, of which 6 were waited for; matrix products, arithmetic and copies ran while one was open for 4% of the time, Pallas kernels for 0%

profile of v1, /device:TPU:32, one launch (start us, length us, event | category | flops | bytes accessed | tf_op | source)
XLA Modules:
  0.0 586.2 jit_solution(11390144644669981370)
XLA Ops:
  7.3 7.6 %all-gather = bf16[256,512]{1,0:T(8,128)(2,1)} all-gather(bf16[128,512]{1,0:T(8,128)(2,1)} %param.14), channel_id=2, replica_groups=mesh['fsdp_0'=2,'fsdp_1'=16,'side'=16] {'fsdp_0'}, dimensions={0}, use_global_device_ids=true | all-gather | bytes 393216 | tf_op jit(solution)/shard_map/all_gather | solution.py:40
  30.1 67.4 %all-gather.4.cloned.1.call-done = bf16[32,128,512]{2,1,0:T(8,128)(2,1)} async-done(((bf16[2,128,512]{2,1,0:T(8,128)(2,1)}), bf16[32,128,512]{2,1,0:T(8,128)(2,1)}) %all-gather.4.cloned.1.call-update) | async-done | bytes 4194320 | tf_op jit(solution)/shard_map/all_gather | solution.py:40
  97.5 2.6 copy.89
  109.8 1.5 pad_maximum_fusion
  111.3 3.9 copy.97
  124.5 2.6 copy.106
  127.1 2.6 maximum_bitcast_fusion
  130.2 2.4 copy.108
  132.6 1.3 copy-done.3
  133.9 1.4 copy.110
  135.3 9.0 %all-to-all-start.2 = ((bf16[128,32,160]{0,2,1:T(8,128)(2,1)}), bf16[128,32,160]{0,2,1:T(8,128)(2,1)S(1)}, u32[]{:S(2)}, u32[]{:S(2)}) async-start(bf16[128,32,160]{0,2,1:T(8,128)(2,1)} %bitcast.50), calls=%async_computation.4 | async-start | bytes 2621440 | tf_op jit(solution)/shard_map/all_to_all | solution.py:192
  144.4 102.8 %reduce-scatter.3.cloned.1.call-done = bf16[2,128,512]{2,1,0:T(8,128)(2,1)} async-done(((bf16[32,128,512]{2,1,0:T(8,128)(2,1)}), bf16[2,128,512]{2,1,0:T(8,128)(2,1)}) %reduce-scatter.3.cloned.1.call-update) | async-done | bytes 262160 | tf_op jit(solution)/shard_map/reduce_scatter | solution.py:57
  247.2 24.0 %reduce-scatter.5.cloned.1.call-done = bf16[1,128,512]{2,1,0:T(8,128)(2,1)} async-done(((bf16[2,128,512]{2,1,0:T(8,128)(2,1)}), bf16[1,128,512]{2,1,0:T(8,128)(2,1)}) %reduce-scatter.5.cloned.1.call-update) | async-done | bytes 131088 | tf_op jit(solution)/shard_map/reduce_scatter | solution.py:57
  271.2 1.4 stack.14
  272.6 201.9 %all_to_all.50 = bf16[32,128,512]{2,1,0:T(8,128)(2,1)S(1)} all-to-all(bf16[32,128,512]{2,1,0:T(8,128)(2,1)S(1)} %stack.14), channel_id=1, replica_groups=mesh['fsdp_0'=2,'fsdp_1'=16,'side'=16] {'fsdp_0','fsdp_1'}, dimensions={0} | all-to-all | bytes 8388608 | tf_op jit(solution)/shard_map/all_to_all | solution.py:28
  474.5 1.9 copy-done.2
  478.0 6.8 %all-to-all-start.3 = ((bf16[16,10,512]{2,1,0:T(8,128)(2,1)}), bf16[16,10,512]{2,1,0:T(8,128)(2,1)S(1)}, u32[]{:S(2)}, u32[]{:S(2)}) async-start(bf16[16,10,512]{2,1,0:T(8,128)(2,1)} %reshape.271), calls=%async_computation.5 | async-start | bytes 524288 | tf_op jit(solution)/shard_map/all_to_all | solution.py:73
  484.8 9.6 %all-to-all-done.3 = bf16[16,10,512]{2,1,0:T(8,128)(2,1)S(1)} async-done(((bf16[16,10,512]{2,1,0:T(8,128)(2,1)}), bf16[16,10,512]{2,1,0:T(8,128)(2,1)S(1)}, u32[]{:S(2)}, u32[]{:S(2)}) %all-to-all-start.3) | async-done | bytes 163872 | tf_op jit(solution)/shard_map/all_to_all | solution.py:73
  495.8 3.5 all-to-all-start.4
  499.4 3.7 fusion.16
  504.4 4.5 all-to-all-done.4
  508.9 4.5 all-to-all-start.1
  514.1 64.1 %all-to-all-done.1 = bf16[32,128,160]{1,2,0:T(8,128)(2,1)S(1)} async-done(((bf16[32,128,160]{1,2,0:T(8,128)(2,1)}), bf16[32,128,160]{1,2,0:T(8,128)(2,1)S(1)}, u32[]{:S(2)}, u32[]{:S(2)}) %all-to-all-start.1) | async-done | bytes 1310752 | tf_op jit(solution)/shard_map/all_to_all | solution.py:221
  578.2 1.4 copy.111
  (126 shorter events, 39.4 us)
Async XLA Ops:
  7.2 14.2 %copy-start = (s32[32]{0:T(128)S(1)}, s32[32]{0:T(128)}, u32[]{:S(2)}) copy-start(s32[32]{0:T(128)} %param.20) | copy-start | bytes 388
  7.2 15.5 %copy-start.16 = (f32[128]{0:T(128)S(1)}, f32[128]{0:T(128)}, u32[]{:S(2)}) copy-start(f32[128]{0:T(128)} %param.16) | copy-start | bytes 1540
  7.2 15.5 %copy-start.17 = (f32[128]{0:T(128)S(1)}, f32[128]{0:T(128)}, u32[]{:S(2)}) copy-start(f32[128]{0:T(128)} %param.17) | copy-start | bytes 1540
  7.2 15.5 %copy-start.4 = (bf16[128,2560]{1,0:T(8,128)(2,1)S(1)}, bf16[128,2560]{1,0:T(8,128)(2,1)}, u32[]{:S(2)}) copy-start(bf16[128,2560]{1,0:T(8,128)(2,1)} %param.15) | copy-start | bytes 1966084
  7.2 90.3 %all-gather.4.cloned.1.call-start = ((), (), s32[]{:S(2)}) async-start(), calls=%async_computation.9 | async-start | bytes 4456448 | tf_op jit(solution)/shard_map/all_gather | solution.py:40
  14.9 232.3 %reduce-scatter.3.cloned.1.call-start = ((), (), s32[]{:S(2)}) async-start(), calls=%async_computation.7 | async-start | bytes 4456448 | tf_op jit(solution)/shard_map/reduce_scatter | solution.py:57
  102.9 1.3 copy-start.10
  104.9 0.9 copy-start.11
  106.6 0.9 copy-start.12
  108.2 0.9 copy-start.13
  117.4 1.2 copy-start.6
  121.0 0.9 copy-start.8
  122.7 0.9 copy-start.9
  132.6 1.3 copy-start.3
  135.3 111.9 %all-to-all-start.2 = ((bf16[128,32,160]{0,2,1:T(8,128)(2,1)}), bf16[128,32,160]{0,2,1:T(8,128)(2,1)S(1)}, u32[]{:S(2)}, u32[]{:S(2)}) async-start(bf16[128,32,160]{0,2,1:T(8,128)(2,1)} %bitcast.50), calls=%async_computation.4 | async-start | bytes 2621440 | tf_op jit(solution)/shard_map/all_to_all | solution.py:192
  144.3 126.9 %reduce-scatter.5.cloned.1.call-start = ((), (), s32[]{:S(2)}) async-start(), calls=%async_computation.8 | async-start | bytes 393216 | tf_op jit(solution)/shard_map/reduce_scatter | solution.py:57
  474.5 1.9 copy-start.2
  476.4 18.0 %copy-start.5 = (bf16[160,512]{1,0:T(8,128)(2,1)S(1)}, bf16[160,512]{1,0:T(8,128)(2,1)}, u32[]{:S(2)}) copy-start(bf16[160,512]{1,0:T(8,128)(2,1)} %param.21) | copy-start | bytes 491524
  476.4 18.0 %copy-start.14 = (bf16[10,512]{1,0:T(8,128)(2,1)S(1)}, bf16[10,512]{1,0:T(8,128)(2,1)}, u32[]{:S(2)}) copy-start(bf16[10,512]{1,0:T(8,128)(2,1)} %param.23) | copy-start | bytes 30724
  476.4 18.0 %copy-start.15 = (bf16[10,512]{1,0:T(8,128)(2,1)S(1)}, bf16[10,512]{1,0:T(8,128)(2,1)}, u32[]{:S(2)}) copy-start(bf16[10,512]{1,0:T(8,128)(2,1)} %param.22) | copy-start | bytes 30724
  478.0 16.4 %all-to-all-start.3 = ((bf16[16,10,512]{2,1,0:T(8,128)(2,1)}), bf16[16,10,512]{2,1,0:T(8,128)(2,1)S(1)}, u32[]{:S(2)}, u32[]{:S(2)}) async-start(bf16[16,10,512]{2,1,0:T(8,128)(2,1)} %reshape.271), calls=%async_computation.5 | async-start | bytes 524288 | tf_op jit(solution)/shard_map/all_to_all | solution.py:73
  495.8 13.1 %all-to-all-start.4 = ((bf16[16,10,512]{2,1,0:T(8,128)(2,1)}), bf16[16,10,512]{2,1,0:T(8,128)(2,1)S(1)}, u32[]{:S(2)}, u32[]{:S(2)}) async-start(bf16[16,10,512]{2,1,0:T(8,128)(2,1)} %broadcast_in_dim.19), calls=%async_computation.6 | async-start | bytes 524288 | tf_op jit(solution)/shard_map/all_to_all | solution.py:79
  508.9 70.8 %copy-start.1 = (s32[32]{0:T(128)S(1)}, s32[32]{0:T(128)}, u32[]{:S(2)}) copy-start(s32[32]{0:T(128)} %param.20) | copy-start | bytes 388
  508.9 69.3 %all-to-all-start.1 = ((bf16[32,128,160]{1,2,0:T(8,128)(2,1)}), bf16[32,128,160]{1,2,0:T(8,128)(2,1)S(1)}, u32[]{:S(2)}, u32[]{:S(2)}) async-start(bf16[32,128,160]{1,2,0:T(8,128)(2,1)} %bitcast.96), calls=%async_computation.3 | async-start | bytes 2621440 | tf_op jit(solution)/shard_map/all_to_all | solution.py:221
  (1 other events, 0.9 us)
Sparse Core Ops, SparseCore 0:
  15.0 82.4 all-gather.3
  132.7 114.4 reduce-scatter.2
  250.0 21.1 reduce-scatter.4
